TPU v7x, 512 devices: a whole 4x8x8 slice. The times are simulated.
512 devices in a mesh: grp: 16 (over y_hi, x, core), chan: 32 (over y_lo, z).
Axes of the slice: x: 4, y: 8 (y_hi: 2, y_lo: 4; y = y_hi * 4 + y_lo), z: 8, core: 2. Of those that a mesh axis runs over, the one named last changes fastest.
Arguments:
- voltages: int32 [1024, 31, 8192], P('grp', None, 'chan'), may hold values from -128 to 127
- plan: int32 [3, 16], replicated, may hold values from 0 to 15, as said below
Outputs:
- visibility: bfloat16 [3, 1024, 2048, 128], P(None, 'grp', 'chan')
Inputs may be any that keep to these rules, and one draw needn't show every extreme that they name: Every row is a perfect matching of the 16 groups: plan[r, plan[r, g]] = g and plan[r, g] != g; the 3 partners of a group are all different.
All inputs are finite; a program needn't handle non-finite values.
Results may differ from a plain program's by a relative error of at most 0.0057.
Values may be sent and summed in bfloat16 or wider, within the bound.
A program may use at most 64 MiB of HBM per device.

v0:
```python
import math

import jax
import jax.numpy as jnp
from jax import lax
from jax.sharding import PartitionSpec as P

TAPS = 16


def taper_coeff(position, length_total, fft_len):
    window = 0.5 - 0.5 * jnp.cos(2.0 * math.pi * position / length_total)
    return window * jnp.sinc((position - 0.5 * length_total) / fft_len)


def correlate(mine_rows, theirs, sig_count, spec_count):
    half_len = mine_rows.shape[1]
    mine_four = mine_rows.reshape(2, half_len, sig_count, spec_count)
    their_four = theirs.reshape(2, half_len, sig_count, spec_count)
    left_side = jnp.concatenate([mine_four[0], mine_four[1]], axis=-1)
    right_re = jnp.concatenate([their_four[0], their_four[1]], axis=-1)
    right_im = jnp.concatenate([-their_four[1], their_four[0]], axis=-1)
    vis_re = jnp.einsum("kas,kbs->akb", left_side, right_re, preferred_element_type=jnp.float32)
    vis_im = jnp.einsum("kas,kbs->akb", left_side, right_im, preferred_element_type=jnp.float32)
    return jnp.concatenate([vis_re, vis_im], axis=-1) * (1.0 / spec_count)


def local(voltages, plan):
    sig_count, frames, block_len = voltages.shape
    chan_count = lax.axis_size("chan")
    group_count = lax.axis_size("grp")
    spec_count = frames - TAPS + 1
    fft_len = block_len * chan_count
    sub_len = block_len // chan_count
    chan_id = lax.axis_index("chan")
    group_id = lax.axis_index("grp")
    highest = lax.Precision.HIGHEST
    n_global = chan_id * block_len + jnp.arange(block_len)
    tap_ids = jnp.arange(TAPS)[:, None]
    coeffs = taper_coeff(
        (tap_ids * fft_len + n_global[None, :]).astype(jnp.float32), TAPS * fft_len, fft_len
    )
    samples = voltages.astype(jnp.float32)

    def add_tap(tap_index, running):
        weight = lax.dynamic_slice_in_dim(coeffs, tap_index, 1, 0)
        return running + weight * lax.dynamic_slice_in_dim(samples, tap_index, spec_count, 1)

    filtered = lax.fori_loop(
        0, TAPS, add_tap, jnp.zeros((sig_count, spec_count, block_len), jnp.float32)
    )
    row_count = sig_count * spec_count
    flat_rows = filtered.reshape(row_count, block_len).T.reshape(1, block_len, row_count)
    turned = lax.all_to_all(flat_rows, "chan", split_axis=1, concat_axis=0, tiled=True)
    src_ids = jnp.arange(chan_count)
    angle_small = (
        2.0
        * math.pi
        * (src_ids[:, None] * src_ids[None, :] % chan_count).astype(jnp.float32)
        / chan_count
    )
    part_re = jnp.einsum("nk,nmr->kmr", jnp.cos(angle_small), turned, precision=highest)
    part_im = -jnp.einsum("nk,nmr->kmr", jnp.sin(angle_small), turned, precision=highest)
    n_second = chan_id * sub_len + jnp.arange(sub_len)
    twist_angle = (
        2.0
        * math.pi
        * (src_ids[:, None] * n_second[None, :] % fft_len).astype(jnp.float32)
        / fft_len
    )
    twist_cos = jnp.cos(twist_angle)[:, :, None]
    twist_sin = jnp.sin(twist_angle)[:, :, None]
    rot_re = part_re * twist_cos + part_im * twist_sin
    rot_im = part_im * twist_cos - part_re * twist_sin
    stacked = jnp.stack([rot_re, rot_im])
    columns = lax.all_to_all(stacked, "chan", split_axis=1, concat_axis=2, tiled=True)
    col_re = columns[0, 0]
    col_im = columns[1, 0]
    ch_dev = block_len // 2
    out_ids = jnp.arange(ch_dev)
    in_ids = jnp.arange(block_len)
    angle_big = (
        2.0
        * math.pi
        * (out_ids[:, None] * in_ids[None, :] % block_len).astype(jnp.float32)
        / block_len
    )
    cos_big = jnp.cos(angle_big)
    sin_big = jnp.sin(angle_big)
    chan_re = jnp.dot(cos_big, col_re, precision=highest) + jnp.dot(
        sin_big, col_im, precision=highest
    )
    chan_im = jnp.dot(cos_big, col_im, precision=highest) - jnp.dot(
        sin_big, col_re, precision=highest
    )
    gain_const = 1.0 / (64.0 * math.sqrt(fft_len))
    channel = (jnp.stack([chan_re, chan_im]) * gain_const).astype(jnp.bfloat16)
    group_ids = jnp.arange(group_count)
    partner = jnp.sum(jnp.where(group_ids[None, :] == group_id, plan, 0), axis=1)
    half_len = ch_dev // 2
    lower_half = channel[:, :half_len]
    upper_half = channel[:, half_len:]
    listed = jnp.any(partner[:, None] == group_ids[None, :], axis=0)
    slot_ids = group_ids[:, None, None, None]
    chosen_half = jnp.where(slot_ids > group_id, upper_half[None], lower_half[None])
    slot_data = jnp.where(listed[:, None, None, None], chosen_half, jnp.zeros_like(chosen_half))
    received = lax.all_to_all(slot_data, "grp", split_axis=0, concat_axis=0, tiled=True)
    results = []
    for round_index in range(plan.shape[0]):
        partner_id = partner[round_index]
        upper_flag = (group_id > partner_id).astype(jnp.int32)
        mine_rows = lax.dynamic_slice_in_dim(channel, upper_flag * half_len, half_len, 1)
        theirs = lax.dynamic_index_in_dim(received, partner_id, 0, keepdims=False)
        results.append(correlate(mine_rows, theirs, sig_count, spec_count))
    return jnp.stack(results).astype(jnp.bfloat16)


def solution(mesh):
    in_specs = (P("grp", None, "chan"), P())
    out_specs = P(None, "grp", "chan", None)
    return jax.shard_map(local, mesh=mesh, in_specs=in_specs, out_specs=out_specs, check_vma=False)
```

profile of v0, /device:TPU:15, one launch (start us, length us, event | category | flops | bytes accessed | tf_op | source)
XLA Modules:
  0.0 277.8 jit_solution(3576166361434823904)
XLA Ops:
  0.0 2.8 copy_convert_fusion
  2.9 8.8 %while.14 = (s32[]{:T(128)}, f32[64,16,256]{2,1,0:T(8,128)S(1)}, f32[16,256]{1,0:T(8,128)S(1)}, f32[64,31,256]{2,1,0:T(8,128)S(1)}, s32[]{:T(128)}, /*index=5*/s32[]{:T(128)}) while((s32[]{:T(128)}, f32[64,16,256]{2,1,0:T(8,128)S(1)}, f32[16,256]{1,0:T(8,128)S(1)}, f32[64,31,256]{2,1,0:T(8,128)S(1)}, s32[]{:T(128)}, ...), condition=%wide.region_3.4_spmd.clone, body=%wide.region_2.3_spmd.clone.sunk | while | flops 786435 | bytes 3148887 | solution.py:49
  3.0 0.5 select_add_fusion.2
  3.5 0.5 select_add_fusion.2
  4.1 0.5 select_add_fusion.2
  4.6 0.5 select_add_fusion.2
  5.2 0.5 select_add_fusion.2
  5.7 0.5 select_add_fusion.2
  6.3 0.5 select_add_fusion.2
  6.8 0.5 select_add_fusion.2
  7.4 0.5 select_add_fusion.2
  7.9 0.5 select_add_fusion.2
  8.5 0.5 select_add_fusion.2
  9.0 0.5 select_add_fusion.2
  9.6 0.5 select_add_fusion.2
  10.1 0.5 select_add_fusion.2
  10.7 0.5 select_add_fusion.2
  11.3 0.5 select_add_fusion.2
  11.8 1.9 copy.113
  13.7 13.4 %all-to-all-start = ((f32[1,256,1024]{2,0,1:T(1,128)}), f32[1,256,1024]{2,0,1:T(1,128)S(1)}, u32[]{:S(2)}, u32[]{:S(2)}) async-start(f32[1,256,1024]{2,0,1:T(1,128)} %copy.113), calls=%async_computation | async-start | bytes 2097152 | tf_op jit(solution)/shard_map/all_to_all | solution.py:54
  27.2 25.9 %all-to-all-done = f32[1,256,1024]{2,0,1:T(1,128)S(1)} async-done(((f32[1,256,1024]{2,0,1:T(1,128)}), f32[1,256,1024]{2,0,1:T(1,128)S(1)}, u32[]{:S(2)}, u32[]{:S(2)}) %all-to-all-start) | async-done | bytes 1048608 | tf_op jit(solution)/shard_map/all_to_all | solution.py:54
  53.3 1.6 convolution_negate_fusion
  54.9 1.8 add_bitcast_fusion
  57.0 2.5 copy.116
  59.5 7.5 %all-to-all-start.1 = ((f32[2,32,8,1024]{3,2,0,1:T(8,128)}), f32[2,32,8,1024]{3,2,0,1:T(8,128)S(1)}, u32[]{:S(2)}, u32[]{:S(2)}) async-start(f32[2,32,8,1024]{3,2,0,1:T(8,128)} %copy.116), calls=%async_computation.1 | async-start | bytes 4194304 | tf_op jit(solution)/shard_map/all_to_all | solution.py:76
  67.3 48.6 %all-to-all-done.1 = f32[2,32,8,1024]{3,2,0,1:T(8,128)S(1)} async-done(((f32[2,32,8,1024]{3,2,0,1:T(8,128)}), f32[2,32,8,1024]{3,2,0,1:T(8,128)S(1)}, u32[]{:S(2)}, u32[]{:S(2)}) %all-to-all-start.1) | async-done | bytes 2097184 | tf_op jit(solution)/shard_map/all_to_all | solution.py:76
  115.9 1.2 fusion.6
  117.1 1.2 fusion.7
  118.3 1.2 fusion.3
  119.5 1.2 fusion.4
  120.8 2.5 select_select_fusion
  123.3 15.5 %all-to-all-start.2 = ((bf16[16,2,64,1024]{3,2,1,0:T(8,128)(2,1)}), bf16[16,2,64,1024]{3,2,1,0:T(8,128)(2,1)}, u32[]{:S(2)}, u32[]{:S(2)}) async-start(bf16[16,2,64,1024]{3,2,1,0:T(8,128)(2,1)} %select_select_fusion), calls=%async_computation.2 | async-start | bytes 8388608 | tf_op jit(solution)/shard_map/all_to_all | solution.py:107
  138.9 0.6 fusion.106
  147.1 0.4 copy.124
  147.6 1.1 copy.125
  148.9 0.4 copy.133
  149.5 0.4 copy.134
  150.0 0.4 copy.142
  150.6 0.4 copy.143
  151.0 94.7 %all-to-all-done.2 = bf16[16,2,64,1024]{3,2,1,0:T(8,128)(2,1)} async-done(((bf16[16,2,64,1024]{3,2,1,0:T(8,128)(2,1)}), bf16[16,2,64,1024]{3,2,1,0:T(8,128)(2,1)}, u32[]{:S(2)}, u32[]{:S(2)}) %all-to-all-start.2) | async-done | bytes 4194336 | tf_op jit(solution)/shard_map/all_to_all | solution.py:107
  245.7 2.0 constant_dynamic-slice_fusion.12
  247.8 1.1 copy.120
  249.1 0.4 copy.121
  249.5 0.7 copy-done.5
  250.2 1.6 convolution_bitcast_fusion.5
  251.9 1.8 convolution_bitcast_fusion.4
  253.8 1.7 copy.154
  255.5 1.3 copy.129
  256.8 1.7 copy.155
  258.6 2.0 copy.130
  260.6 1.0 neg.19
  261.6 2.8 convolution_bitcast_fusion.3
  264.3 1.8 convolution_bitcast_fusion.2
  266.2 1.1 copy.157
  267.8 0.4 copy.139
  268.3 0.5 convolution_bitcast_fusion.1
  268.8 0.5 convolution_bitcast_fusion
  269.2 1.1 copy-done
  270.3 0.6 fusion
  271.0 1.0 copy-done.1
  271.9 0.6 copy-done.2
  272.6 0.6 fusion.1
  273.2 0.6 fusion.2
  274.1 3.7 %copy.146 = bf16[3,64,64,128]{3,2,1,0:T(8,128)(2,1)} copy(bf16[3,64,64,128]{3,1,2,0:T(8,128)(2,1)S(1)} %pad_maximum_fusion) | data formatting | bytes 6291456 | tf_op jit(solution)/shard_map/stack | solution.py:115
  (53 shorter events, 3.7 us)
Async XLA Ops:
  13.7 39.4 %all-to-all-start = ((f32[1,256,1024]{2,0,1:T(1,128)}), f32[1,256,1024]{2,0,1:T(1,128)S(1)}, u32[]{:S(2)}, u32[]{:S(2)}) async-start(f32[1,256,1024]{2,0,1:T(1,128)} %copy.113), calls=%async_computation | async-start | bytes 2097152 | tf_op jit(solution)/shard_map/all_to_all | solution.py:54
  59.5 7.6 %copy-start.6 = (s32[3,16]{1,0:T(4,128)S(1)}, s32[3,16]{1,0:T(4,128)}, u32[]{:S(2)}) copy-start(s32[3,16]{1,0:T(4,128)} %param.5) | copy-start | bytes 580
  59.5 56.4 %all-to-all-start.1 = ((f32[2,32,8,1024]{3,2,0,1:T(8,128)}), f32[2,32,8,1024]{3,2,0,1:T(8,128)S(1)}, u32[]{:S(2)}, u32[]{:S(2)}) async-start(f32[2,32,8,1024]{3,2,0,1:T(8,128)} %copy.116), calls=%async_computation.1 | async-start | bytes 4194304 | tf_op jit(solution)/shard_map/all_to_all | solution.py:76
  123.3 122.4 %all-to-all-start.2 = ((bf16[16,2,64,1024]{3,2,1,0:T(8,128)(2,1)}), bf16[16,2,64,1024]{3,2,1,0:T(8,128)(2,1)}, u32[]{:S(2)}, u32[]{:S(2)}) async-start(bf16[16,2,64,1024]{3,2,1,0:T(8,128)(2,1)} %select_select_fusion), calls=%async_computation.2 | async-start | bytes 8388608 | tf_op jit(solution)/shard_map/all_to_all | solution.py:107
  249.5 0.7 copy-start.5
  250.2 1.7 copy-start.3
  250.2 1.7 copy-start.4
  268.7 1.6 copy-start
  270.3 1.6 copy-start.1
  270.3 2.2 copy-start.2
where the time goes:
time: 279 us; the launch traced here: 278 us
  waiting for transfers between devices  169 us (61%)
  starting transfers between devices  36.5 us (13%)
  local copies, waits for them, and re-layouts  29.2 us (10%)
  other arithmetic  17.6 us (6%)
  matrix products  17.1 us (6%)
  between operations  7.73 us (3%)
    all_to_all x1, waiting for transfers between devices, local(): lax.all_to_all(slot_data, 'grp', split_axis=0, concat_axis=0, tiled=True)  94.7 us
    all_to_all x1, waiting for transfers between devices, local(): lax.all_to_all(stacked, 'chan', split_axis=1, concat_axis=2, tiled=True)  48.6 us
    all_to_all x1, waiting for transfers between devices, local(): lax.all_to_all(flat_rows, 'chan', split_axis=1, concat_axis=0, tiled=True)  25.9 us
    all_to_all x1, starting transfers between devices, local(): lax.all_to_all(slot_data, 'grp', split_axis=0, concat_axis=0, tiled=True)  15.5 us
    all_to_all x1, starting transfers between devices, local(): lax.all_to_all(flat_rows, 'chan', split_axis=1, concat_axis=0, tiled=True)  13.4 us
    unnamed x21, local copies, waits for them, and re-layouts  8.66 us
    add x16, other arithmetic, add_tap(): running + weight * lax.dynamic_slice_in_dim(samples, tap_index, spec_coun...  8.21 us
    all_to_all x1, starting transfers between devices, local(): lax.all_to_all(stacked, 'chan', split_axis=1, concat_axis=2, tiled=True)  7.54 us
  transfers between devices with their start and end apart: 3, of which 3 were waited for; matrix products, arithmetic and copies ran while one was open for 2% of the time, Pallas kernels for 0%

commit v1 on v0

v1 whole, which is shorter than its diff:
```python
import functools
import math

import jax
import jax.numpy as jnp
import numpy as np
from jax import lax
from jax.experimental import pallas as pl
from jax.experimental.pallas import tpu as pltpu
from jax.sharding import PartitionSpec as P

TAPS = 16
MESH = pl.DeviceIdType.MESH
F32 = jnp.float32
BF16 = jnp.bfloat16


def coeff_table(fft_len, n_chan):
    position = np.arange(TAPS * fft_len, dtype=np.float64)
    length = TAPS * fft_len
    window = 0.5 - 0.5 * np.cos(2.0 * np.pi * position / length)
    coeff = window * np.sinc((position - 0.5 * length) / fft_len)
    block = fft_len // n_chan
    table = coeff.reshape(TAPS, n_chan, block).transpose(1, 0, 2)
    return np.ascontiguousarray(table.astype(np.float32))


def twiddle_table(fft_len, n_chan):
    block = fft_len // n_chan
    c = np.arange(n_chan // 2 + 1)[:, None]
    m = np.arange(block)[None, :]
    angle = 2.0 * np.pi * (c * m) / fft_len
    return np.stack([np.cos(angle), np.sin(angle)], 1).astype(np.float32)


def second_matrix(fft_len, block):
    half = block // 4
    m = np.arange(block)[:, None]
    j = np.arange(block // 2)[None, :]
    theta = 2.0 * np.pi * (m * j % block) / block
    phi = 2.0 * np.pi * (m * (j + 1) % block) / block
    re = np.concatenate([np.cos(theta), np.sin(theta)], 0)
    im = np.concatenate([-np.sin(theta), np.cos(theta)], 0)
    re_mirror = np.concatenate([np.cos(phi), -np.sin(phi)], 0)
    im_mirror = np.concatenate([-np.sin(phi), -np.cos(phi)], 0)
    parts = []
    for real, imag in ((re, im), (re_mirror, im_mirror)):
        for lo in (0, half):
            parts.append(real[:, lo : lo + half])
            parts.append(imag[:, lo : lo + half])
    full = np.concatenate(parts, 1) / (64.0 * math.sqrt(fft_len))
    high = full.astype(np.float32).astype(BF16)
    low = (full - high.astype(np.float64)).astype(np.float32).astype(BF16)
    return high, low


def real_dft(x):
    n = len(x)
    if n == 1:
        return [(x[0], None)]
    if n == 2:
        return [(x[0] + x[1], None), (x[0] - x[1], None)]
    even = real_dft(x[0::2])
    odd = real_dft(x[1::2])
    out = [None] * (n // 2 + 1)
    out[0] = (even[0][0] + odd[0][0], None)
    out[n // 2] = (even[0][0] - odd[0][0], None)
    quarter = n // 4
    out[quarter] = (even[quarter][0], -odd[quarter][0])
    for c in range(1, quarter):
        er, ei = even[c]
        orr, oi = odd[c]
        angle = 2.0 * math.pi * c / n
        wr, wi = math.cos(angle), -math.sin(angle)
        if 8 * c == n:
            tr, ti = (orr + oi) * wr, (oi - orr) * wr
        else:
            tr, ti = orr * wr - oi * wi, orr * wi + oi * wr
        out[c] = (er + tr, ei + ti)
        out[n // 2 - c] = (er - tr, ti - ei)
    return out


def exchange_kernel(
    dims,
    v_ref, coeff_ref, tw_ref, bh_ref, bl_ref,
    own_ref, slots_ref,
    coeff, filt, r1, zh, zl, s2, r2, r2x, t32, t32x, tn, tx,
    coeff_sem, send1, recv1, send2, recv2, send2x, recv2x, local_sem, sendq, recvq, relay_sem, relayq,
):
    n_chan, plane, sig, spec, block = dims
    me = lax.axis_index("chan")
    gid = lax.axis_index("grp")
    other = lax.rem(gid + plane, 2 * plane)
    y_hi = gid // plane
    x = lax.rem(gid, plane) // 2
    core = lax.rem(gid, 2)
    n_x = plane // 2
    sib = y_hi * plane + x * 2 + (1 - core)
    barrier = pltpu.get_barrier_semaphore()

    def greet(k, carry):
        peer = lax.rem(me + k, n_chan)

        @pl.when(k > 0)
        def _():
            pl.semaphore_signal(barrier, inc=1, device_id={"chan": peer}, device_id_type=MESH)

        pl.semaphore_signal(
            barrier, inc=1, device_id={"grp": other, "chan": peer}, device_id_type=MESH
        )
        return carry

    lax.fori_loop(0, n_chan, greet, 0)
    for dx in range(1, n_x):
        dest = y_hi * plane + lax.rem(x + dx, n_x) * 2 + core
        pl.semaphore_signal(barrier, inc=1, device_id={"grp": dest}, device_id_type=MESH)
    pl.semaphore_signal(barrier, inc=1, device_id={"grp": sib}, device_id_type=MESH)

    load = pltpu.make_async_copy(coeff_ref.at[me], coeff, coeff_sem)
    load.start()
    load.wait()

    def fir(s, carry):
        for lane in range(0, block, 128):
            lanes = pl.ds(lane, 128)
            total = None
            for t in range(TAPS):
                term = coeff[t : t + 1, lanes] * v_ref[s + t, :, lanes]
                total = term if total is None else total + term
            filt[2 * s, :, lanes] = total[: sig // 2].astype(BF16)
            filt[2 * s + 1, :, lanes] = total[sig // 2 :].astype(BF16)
        return carry

    lax.fori_loop(0, spec, fir, 0)
    pl.semaphore_wait(barrier, 2 * n_chan - 1 + n_x)

    def copy1(src, dest):
        return pltpu.make_async_remote_copy(
            src_ref=filt.at[dest], dst_ref=r1.at[src], send_sem=send1.at[dest], recv_sem=recv1.at[src],
            device_id={"chan": dest}, device_id_type=MESH,
        )

    def start1(k, carry):
        copy1(me, lax.rem(me + k, n_chan)).start()
        return carry

    lax.fori_loop(1, n_chan, start1, 0)
    mine1 = pltpu.make_async_copy(filt.at[me], r1.at[me], local_sem.at[0])
    mine1.start()
    mine1.wait()

    def wait1(k, carry):
        peer = lax.rem(me + k, n_chan)
        copy1(peer, peer).wait_recv()
        return carry

    lax.fori_loop(1, n_chan, wait1, 0)

    rows = sig * spec // n_chan
    n_half = n_chan // 2

    def first(p, carry):
        row = pl.multiple_of((p // 2) * 16, 16)
        lane = pl.multiple_of(lax.rem(p, 2) * 128, 128)
        samples = [r1[d, pl.ds(row, 16), pl.ds(lane, 128)].astype(F32) for d in range(n_chan)]
        for c, (re, im) in enumerate(real_dft(samples)):
            cos = tw_ref[c, 0:1, pl.ds(lane, 128)]
            sin = tw_ref[c, 1:2, pl.ds(lane, 128)]
            if im is None:
                zr, zi = re * cos, -(re * sin)
            else:
                zr, zi = re * cos + im * sin, im * cos - re * sin
            for base, z in ((0, zr), (block, zi)):
                lanes = pl.ds(pl.multiple_of(base + lane, 128), 128)
                high = z.astype(BF16)
                zh[c, pl.ds(row, 16), lanes] = high
                zl[c, pl.ds(row, 16), lanes] = (z - high.astype(F32)).astype(BF16)
        return carry

    lax.fori_loop(0, (rows // 16) * (block // 128), first, 0)

    for lo, hi in ((0, n_half // 2 + 1), (n_half // 2 + 1, n_half + 1)):
        count = (hi - lo) * rows
        left_h = zh[lo:hi].reshape(count, 2 * block)
        left_l = zl[lo:hi].reshape(count, 2 * block)
        out = jnp.dot(left_h, bh_ref[...], preferred_element_type=F32)
        out += jnp.dot(left_h, bl_ref[...], preferred_element_type=F32)
        out += jnp.dot(left_l, bh_ref[...], preferred_element_type=F32)
        for c in range(lo, hi):
            part = out[(c - lo) * rows : (c - lo + 1) * rows].astype(BF16)
            s2[c, 0] = part[:, 0:128]
            s2[c, 1] = part[:, 128:256]
            if 0 < c < n_half:
                s2[n_chan - c, 0] = part[:, 256:384]
                s2[n_chan - c, 1] = part[:, 384:512]

    def copy2(src, dest):
        return pltpu.make_async_remote_copy(
            src_ref=s2.at[dest], dst_ref=r2.at[src], send_sem=send2.at[dest], recv_sem=recv2.at[src],
            device_id={"chan": dest}, device_id_type=MESH,
        )

    def copy2x(src, dest):
        return pltpu.make_async_remote_copy(
            src_ref=s2.at[dest, 1 - y_hi], dst_ref=r2x.at[src],
            send_sem=send2x.at[dest], recv_sem=recv2x.at[src],
            device_id={"grp": other, "chan": dest}, device_id_type=MESH,
        )

    def start2(k, carry):
        dest = lax.rem(me + k, n_chan)

        @pl.when(k > 0)
        def _():
            copy2(me, dest).start()

        copy2x(me, dest).start()
        return carry

    lax.fori_loop(0, n_chan, start2, 0)
    mine2 = pltpu.make_async_copy(s2.at[me], r2.at[me], local_sem.at[0])
    mine2.start()
    mine2.wait()

    def wait2(k, carry):
        peer = lax.rem(me + k, n_chan)
        copy2(peer, peer).wait_recv()
        return carry

    lax.fori_loop(1, n_chan, wait2, 0)
    low_lane = lax.broadcasted_iota(jnp.int32, (sig, 128), 1) < 64

    def swap(a, b):
        re = jnp.where(low_lane, a, pltpu.roll(b, 64, 1))
        im = jnp.where(low_lane, pltpu.roll(a, 64, 1), b)
        return jnp.concatenate([re, im], 0).T

    def turn(s, carry):
        low = r2[pl.ds(2 * s, 2), 0].reshape(sig, 128).astype(F32)
        high = r2[pl.ds(2 * s, 2), 1].reshape(sig, 128).astype(F32)
        t32[pl.ds(s, 128, stride=spec), :] = swap(low, high)
        return carry

    lax.fori_loop(0, spec, turn, 0)

    def pack(i, carry):
        row = pl.multiple_of(i * 128, 128)
        tn[pl.ds(i * 8, 8)] = t32[pl.ds(row, 128), :].reshape(8, spec, 128).astype(BF16)
        return carry

    lax.fori_loop(0, 16, pack, 0)

    def copyq(src_ref, slot, sem, dest_grp):
        return pltpu.make_async_remote_copy(
            src_ref=src_ref, dst_ref=slots_ref.at[slot], send_sem=sem, recv_sem=recvq.at[slot],
            device_id={"grp": dest_grp}, device_id_type=MESH,
        )

    sends = []
    for dx in range(1, n_x):
        dest_x = lax.rem(x + dx, n_x)
        dest = y_hi * plane + dest_x * 2 + core
        upper = (dest_x > x).astype(jnp.int32)
        sends.append(copyq(tn.at[pl.ds(upper * 64, 64)], gid, sendq.at[dx - 1], dest))
        sends[-1].start()
    sends.append(copyq(tn.at[pl.ds((1 - core) * 64, 64)], gid, sendq.at[n_x - 1], sib))
    sends[-1].start()
    keep = pltpu.make_async_copy(tn, own_ref, local_sem.at[0])
    keep.start()

    def wait2x(k, carry):
        peer = lax.rem(me + k, n_chan)
        copy2x(peer, peer).wait_recv()
        return carry

    lax.fori_loop(0, n_chan, wait2x, 0)

    def turnx(i, carry):
        first_s = r2x[pl.ds(4 * i, 2)].reshape(sig, 128).astype(F32)
        second_s = r2x[pl.ds(4 * i + 2, 2)].reshape(sig, 128).astype(F32)
        both = swap(first_s, second_s)
        t32x[pl.ds(2 * i, 64, stride=spec), :] = both[:64]
        t32x[pl.ds(2 * i + 1, 64, stride=spec), :] = both[64:]
        return carry

    lax.fori_loop(0, spec // 2, turnx, 0)

    def packx(i, carry):
        row = pl.multiple_of(i * 128, 128)
        tx[pl.ds(i * 8, 8)] = t32x[pl.ds(row, 128), :].reshape(8, spec, 128).astype(BF16)
        return carry

    lax.fori_loop(0, 8, packx, 0)
    for dx in range(1, n_x):
        dest = y_hi * plane + lax.rem(x + dx, n_x) * 2 + core
        sends.append(copyq(tx, other, sendq.at[n_x + dx - 1], dest))
        sends[-1].start()
    sends.append(copyq(tx, other, sendq.at[2 * n_x - 1], sib))
    sends[-1].start()
    keepx = pltpu.make_async_copy(tx, slots_ref.at[other], local_sem.at[1])
    keepx.start()

    relays = []
    for part in range(2):
        for dx in range(1, n_x):
            source = lax.rem(y_hi + part, 2) * plane + lax.rem(x + n_x - dx, n_x) * 2 + core
            copyq(tx, source, sendq.at[0], sib).wait_recv()
            relays.append(copyq(slots_ref.at[source], source, relay_sem.at[part * (n_x - 1) + dx - 1], sib))
            relays[-1].start()
    for part in range(2):
        for dx in range(n_x):
            slot = lax.rem(y_hi + part, 2) * plane + lax.rem(x + dx, n_x) * 2 + (1 - core)
            copyq(tx, slot, sendq.at[0], sib).wait_recv()
    keep.wait()
    keepx.wait()
    for item in sends + relays:
        item.wait_send()

    def drain(k, carry):
        dest = lax.rem(me + k, n_chan)

        @pl.when(k > 0)
        def _():
            copy1(me, dest).wait_send()
            copy2(me, dest).wait_send()

        copy2x(me, dest).wait_send()
        return carry

    lax.fori_loop(0, n_chan, drain, 0)


def correlate_kernel(spec, pick_ref, own_ref, other_ref, out_ref, total):
    count = own_ref.shape[0]
    low_lane = lax.broadcasted_iota(jnp.int32, (spec, 128), 1) < 64
    for j in range(count):
        mine = own_ref[j].astype(F32)
        theirs = other_ref[0, j].astype(F32)
        left = jnp.concatenate([mine, pltpu.roll(mine, 64, 1)], 0)[:, :64].astype(BF16)
        right = jnp.concatenate(
            [jnp.where(low_lane, theirs, -theirs), pltpu.roll(theirs, 64, 1)], 0
        ).astype(BF16)
        product = lax.dot_general(left, right, (((0,), (0,)), ((), ())), preferred_element_type=F32)
        total[pl.ds(j, 64, stride=count), :] = product * (1.0 / spec)
    out_ref[0] = total[...].reshape(64, count, 128).astype(BF16)


def solution(mesh):
    n_chan = mesh.shape["chan"]
    n_grp = mesh.shape["grp"]
    plane = n_grp // 2
    n_x = plane // 2

    def local(voltages, plan):
        sig, frames, block = voltages.shape
        spec = frames - TAPS + 1
        fft_len = block * n_chan
        rows = sig * spec // n_chan
        n_c = n_chan // 2 + 1
        rounds = plan.shape[0]
        table = jnp.asarray(coeff_table(fft_len, n_chan))
        twiddle = jnp.asarray(twiddle_table(fft_len, n_chan))
        high, low = second_matrix(fft_len, block)
        frames_first = voltages.transpose(1, 0, 2).astype(F32)
        vmem = pl.BlockSpec(memory_space=pltpu.VMEM)
        anyspace = pl.BlockSpec(memory_space=pl.ANY)
        dma = pltpu.SemaphoreType.DMA
        own, slots = pl.pallas_call(
            functools.partial(exchange_kernel, (n_chan, plane, sig, spec, block)),
            out_shape=(
                jax.ShapeDtypeStruct((128, spec, 128), BF16),
                jax.ShapeDtypeStruct((n_grp, 64, spec, 128), BF16),
            ),
            in_specs=[vmem, anyspace, vmem, vmem, vmem],
            out_specs=(anyspace, anyspace),
            scratch_shapes=[
                pltpu.VMEM((TAPS, block), F32),
                pltpu.VMEM((n_chan, rows, block), BF16),
                pltpu.VMEM((n_chan, rows, block), BF16),
                pltpu.VMEM((n_c, rows, 2 * block), BF16),
                pltpu.VMEM((n_c, rows, 2 * block), BF16),
                pltpu.VMEM((n_chan, 2, rows, 128), BF16),
                pltpu.VMEM((n_chan, 2, rows, 128), BF16),
                pltpu.VMEM((n_chan, rows, 128), BF16),
                pltpu.VMEM((128 * spec, 128), F32),
                pltpu.VMEM((64 * spec, 128), F32),
                pltpu.VMEM((128, spec, 128), BF16),
                pltpu.VMEM((64, spec, 128), BF16),
                dma, dma((n_chan,)), dma((n_chan,)), dma((n_chan,)), dma((n_chan,)),
                dma((n_chan,)), dma((n_chan,)), dma((2,)), dma((2 * n_x,)), dma((n_grp,)),
                dma((2 * n_x,)), dma,
            ],
            compiler_params=pltpu.CompilerParams(
                collective_id=0, has_side_effects=True, vmem_limit_bytes=48 * 1024 * 1024
            ),
            cost_estimate=pl.CostEstimate(
                flops=10**9, bytes_accessed=10**7, transcendentals=0
            ),
        )(frames_first, table, twiddle, jnp.asarray(high), jnp.asarray(low))
        gid = lax.axis_index("grp")
        partner = lax.dynamic_index_in_dim(plan, gid, 1, keepdims=False)
        pick = jnp.stack([partner, (gid > partner).astype(jnp.int32)])
        step = 16
        return pl.pallas_call(
            functools.partial(correlate_kernel, spec),
            out_shape=jax.ShapeDtypeStruct((rounds, sig, 64, 2 * sig), BF16),
            grid_spec=pltpu.PrefetchScalarGridSpec(
                num_scalar_prefetch=1,
                grid=(rounds, 64 // step),
                in_specs=[
                    pl.BlockSpec((step, spec, 128), lambda r, i, p: (p[1, r] * (64 // step) + i, 0, 0)),
                    pl.BlockSpec((1, step, spec, 128), lambda r, i, p: (p[0, r], i, 0, 0)),
                ],
                out_specs=pl.BlockSpec((1, sig, step, 2 * sig), lambda r, i, p: (r, 0, i, 0)),
                scratch_shapes=[pltpu.VMEM((sig * step, 128), F32)],
            ),
        )(pick, own, slots)

    in_specs = (P("grp", None, "chan"), P())
    out_specs = P(None, "grp", "chan", None)
    return jax.shard_map(local, mesh=mesh, in_specs=in_specs, out_specs=out_specs, check_vma=False)
```

time: 279 us -> 99.2 us (0.36)
  the two profiles are of different devices: /device:TPU:15 before, /device:TPU:9 now
where the time goes in v1:
time: 99.2 us; the launch traced here: 98.5 us
  Pallas kernels  94.3 us (95%)
  other arithmetic  2.45 us (2%)
  local copies, waits for them, and re-layouts  1.73 us (2%)
    pallas_call x1, Pallas kernels, local(): pl.pallas_call(functools.partial(exchange_kernel, (n_chan, plane, sig, sp...  83.5 us
    pallas_call x1, Pallas kernels, local(): pl.pallas_call(functools.partial(correlate_kernel, spec), out_shape=jax.S...  10.8 us

profile of v1, /device:TPU:9, one launch (start us, length us, event | category | flops | bytes accessed | tf_op | source)
XLA Modules:
  0.0 98.5 jit_solution(15906505357922361555)
XLA Ops:
  0.0 0.0 copy-start
  0.0 0.7 copy-done
  0.7 0.2 dynamic-slice_reduce_fusion
  0.9 0.6 pad_add_fusion.pick_ref
  1.4 0.0 copy-start.2
  1.4 0.0 copy-start.3
  1.4 0.0 copy-start.4
  1.4 0.0 copy-start.5
  1.4 1.9 %convert_bitcast_fusion.v_ref = f32[31,64,256]{2,1,0:T(8,128)S(1)} fusion(s32[64,31,256]{2,0,1:T(8,128)} %param.6), kind=kLoop, calls=%fused_computation | loop fusion | flops 507904 | bytes 4063232 | tf_op jit(solution)/shard_map/convert_element_type | solution.py:365
  3.3 0.0 copy-done.2
  3.4 0.0 copy-done.3
  3.4 0.0 copy-done.4
  3.4 0.0 copy-done.5
  3.4 83.5 %shard_map.64 = (bf16[128,16,128]{2,1,0:T(8,128)(2,1)S(1)}, bf16[16,64,16,128]{3,2,1,0:T(8,128)(2,1)}) custom-call(f32[31,64,256]{2,1,0:T(8,128)S(1)} %convert_bitcast_fusion.v_ref, f32[32,16,256]{2,1,0:T(8,128)S(1)} %copy-done.4, f32[17,2,256]{2,1,0:T(2,128)S(1)} %copy-done.5, bf16[512,512]{1,0:T(8,128)(2,1)S(1)} %copy-done.3, bf16[512,512]{1,0:T(8,128)(2,1)S(1)} %copy-done.2), custom_call_target="tpu_custom_call" | custom-call | flops 1000000000 | bytes 10000000 | tf_op jit(solution)/shard_map/pallas_call | solution.py:369
  86.9 0.0 copy-start.1
  86.9 0.8 copy-done.1
  87.7 10.8 %shard_map.65 = bf16[3,64,64,128]{3,2,1,0:T(8,128)(2,1)} custom-call(s32[2,3]{1,0:T(2,128)} %pad_add_fusion.pick_ref, bf16[128,16,128]{2,1,0:T(8,128)(2,1)} %copy-done.1, bf16[16,64,16,128]{3,2,1,0:T(8,128)(2,1)} %get-tuple-element.8.other_ref), custom_call_target="tpu_custom_call" | custom-call | tf_op jit(solution)/shard_map/pallas_call | solution.py:405
  (1 shorter events, 0.0 us)
Async XLA Ops:
  0.0 0.7 copy-start
  1.4 1.9 %copy-start.2 = (bf16[512,512]{1,0:T(8,128)(2,1)S(1)}, bf16[512,512]{1,0:T(8,128)(2,1)}, u32[]{:S(2)}) copy-start(bf16[512,512]{1,0:T(8,128)(2,1)} %constant.23.clone.bl_ref) | copy-start | bytes 1572868
  1.4 1.9 %copy-start.3 = (bf16[512,512]{1,0:T(8,128)(2,1)S(1)}, bf16[512,512]{1,0:T(8,128)(2,1)}, u32[]{:S(2)}) copy-start(bf16[512,512]{1,0:T(8,128)(2,1)} %constant.22.clone.bh_ref) | copy-start | bytes 1572868
  1.4 2.0 %copy-start.4 = (f32[32,16,256]{2,1,0:T(8,128)S(1)}, f32[32,16,256]{2,1,0:T(8,128)}, u32[]{:S(2)}) copy-start(f32[32,16,256]{2,1,0:T(8,128)} %constant.20.clone.coeff_ref) | copy-start | bytes 1572868
  1.4 2.0 %copy-start.5 = (f32[17,2,256]{2,1,0:T(2,128)S(1)}, f32[17,2,256]{2,1,0:T(2,128)}, u32[]{:S(2)}) copy-start(f32[17,2,256]{2,1,0:T(2,128)} %constant.21.clone.tw_ref) | copy-start | bytes 104452
  86.9 0.8 copy-start.1

commit v2 on v1

v2 whole, which is shorter than its diff:
```python
import functools
import math

import jax
import jax.numpy as jnp
import numpy as np
from jax import lax
from jax.experimental import pallas as pl
from jax.experimental.pallas import tpu as pltpu
from jax.sharding import PartitionSpec as P

TAPS = 16
MESH = pl.DeviceIdType.MESH
F32 = jnp.float32
BF16 = jnp.bfloat16


def coeff_table(fft_len, n_chan):
    position = np.arange(TAPS * fft_len, dtype=np.float64)
    length = TAPS * fft_len
    window = 0.5 - 0.5 * np.cos(2.0 * np.pi * position / length)
    coeff = window * np.sinc((position - 0.5 * length) / fft_len)
    block = fft_len // n_chan
    table = coeff.reshape(TAPS, n_chan, block).transpose(1, 0, 2)
    return np.ascontiguousarray(table.astype(np.float32))


def twiddle_table(fft_len, n_chan):
    block = fft_len // n_chan
    c = np.arange(n_chan // 2 + 1)[:, None]
    m = np.arange(block)[None, :]
    angle = 2.0 * np.pi * (c * m) / fft_len
    return np.stack([np.cos(angle), np.sin(angle)], 1).astype(np.float32)


def second_matrix(fft_len, block):
    half = block // 4
    m = np.arange(block)[:, None]
    j = np.arange(block // 2)[None, :]
    theta = 2.0 * np.pi * (m * j % block) / block
    phi = 2.0 * np.pi * (m * (j + 1) % block) / block
    re = np.concatenate([np.cos(theta), np.sin(theta)], 0)
    im = np.concatenate([-np.sin(theta), np.cos(theta)], 0)
    re_mirror = np.concatenate([np.cos(phi), -np.sin(phi)], 0)
    im_mirror = np.concatenate([-np.sin(phi), -np.cos(phi)], 0)
    parts = []
    for real, imag in ((re, im), (re_mirror, im_mirror)):
        for lo in (0, half):
            parts.append(real[:, lo : lo + half])
            parts.append(imag[:, lo : lo + half])
    full = np.concatenate(parts, 1) / (64.0 * math.sqrt(fft_len))
    high = full.astype(np.float32).astype(BF16)
    low = (full - high.astype(np.float64)).astype(np.float32).astype(BF16)
    return high, low


def real_dft(x):
    n = len(x)
    if n == 1:
        return [(x[0], None)]
    if n == 2:
        return [(x[0] + x[1], None), (x[0] - x[1], None)]
    even = real_dft(x[0::2])
    odd = real_dft(x[1::2])
    out = [None] * (n // 2 + 1)
    out[0] = (even[0][0] + odd[0][0], None)
    out[n // 2] = (even[0][0] - odd[0][0], None)
    quarter = n // 4
    out[quarter] = (even[quarter][0], -odd[quarter][0])
    for c in range(1, quarter):
        er, ei = even[c]
        orr, oi = odd[c]
        angle = 2.0 * math.pi * c / n
        wr, wi = math.cos(angle), -math.sin(angle)
        if 8 * c == n:
            tr, ti = (orr + oi) * wr, (oi - orr) * wr
        else:
            tr, ti = orr * wr - oi * wi, orr * wi + oi * wr
        out[c] = (er + tr, ei + ti)
        out[n // 2 - c] = (er - tr, ti - ei)
    return out


def exchange_kernel(
    dims,
    v_ref, coeff_ref, tw_ref, bh_ref, bl_ref,
    left_ref, slots_ref,
    volts, vf, coeff, tw, bh, bl, filt, r1, zh, zl, s2, r2, r2x, t32, t32x, tn, tx, left,
    load_sem, send1, recv1, send2, recv2, send2x, recv2x, keep_sem, sendq, recvq, relay_sem,
):
    n_chan, plane, sig, spec, block, chunks = dims
    part = spec // chunks
    quarters = n_chan // part
    rows = sig // quarters
    me = lax.axis_index("chan")
    gid = lax.axis_index("grp")
    other = lax.rem(gid + plane, 2 * plane)
    y_hi = gid // plane
    x = lax.rem(gid, plane) // 2
    core = lax.rem(gid, 2)
    n_x = plane // 2
    sib = y_hi * plane + x * 2 + (1 - core)
    loads = [
        pltpu.make_async_copy(v_ref, volts, load_sem.at[0]),
        pltpu.make_async_copy(coeff_ref.at[me], coeff, load_sem.at[1]),
        pltpu.make_async_copy(tw_ref, tw, load_sem.at[2]),
        pltpu.make_async_copy(bh_ref, bh, load_sem.at[3]),
        pltpu.make_async_copy(bl_ref, bl, load_sem.at[4]),
    ]
    for item in loads:
        item.start()
    barrier = pltpu.get_barrier_semaphore()

    def greet(k, carry):
        peer = lax.rem(me + k, n_chan)

        @pl.when(k > 0)
        def _():
            pl.semaphore_signal(barrier, inc=1, device_id={"chan": peer}, device_id_type=MESH)

        pl.semaphore_signal(
            barrier, inc=1, device_id={"grp": other, "chan": peer}, device_id_type=MESH
        )
        return carry

    lax.fori_loop(0, n_chan, greet, 0)
    for dx in range(1, n_x):
        dest = y_hi * plane + lax.rem(x + dx, n_x) * 2 + core
        pl.semaphore_signal(barrier, inc=1, device_id={"grp": dest}, device_id_type=MESH)
    pl.semaphore_signal(barrier, inc=1, device_id={"grp": sib}, device_id_type=MESH)

    loads[1].wait()
    loads[0].wait()

    def widen(lo, hi):
        def body(t, carry):
            vf[t] = volts[t].astype(F32)
            return carry

        lax.fori_loop(lo, hi, body, 0)

    def peer_of(k):
        step = lax.rem(k, 8)
        hop = (step // 2 + 1) * (1 - 2 * lax.rem(step, 2)) * (1 - step // 7)
        z = lax.rem(lax.rem(me, 8) + hop + 8, 8)
        y = lax.rem(me // 8 + k + k // 8, n_chan // 8)
        return y * 8 + z

    def fir(chunk):
        def body(s, carry):
            for lane in range(0, block, 128):
                lanes = pl.ds(lane, 128)
                total = None
                for t in range(TAPS):
                    term = coeff[t : t + 1, lanes] * vf[chunk * part + s + t, :, lanes]
                    total = term if total is None else total + term
                for q in range(quarters):
                    filt[chunk, quarters * s + q, :, lanes] = total[q * rows : (q + 1) * rows].astype(BF16)
            return carry

        lax.fori_loop(0, part, body, 0)

    def copy1(chunk, src, dest):
        return pltpu.make_async_remote_copy(
            src_ref=filt.at[chunk, dest], dst_ref=r1.at[chunk, src],
            send_sem=send1.at[chunk, dest], recv_sem=recv1.at[chunk, src],
            device_id={"chan": dest}, device_id_type=MESH,
        )

    def start1(chunk):
        def body(k, carry):
            dest = peer_of(k)

            @pl.when(dest != me)
            def _():
                copy1(chunk, me, dest).start()

            return carry

        lax.fori_loop(0, n_chan, body, 0)
        pltpu.make_async_copy(filt.at[chunk, me], r1.at[chunk, me], recv1.at[chunk, me]).start()

    widen(0, part + TAPS - 1)
    fir(0)
    pl.semaphore_wait(barrier, 2 * n_chan - 1 + n_x)
    start1(0)
    for chunk in range(1, chunks):
        widen(chunk * part + TAPS - 1, (chunk + 1) * part + TAPS - 1)
        fir(chunk)
        start1(chunk)

    n_half = n_chan // 2

    def copy2(chunk, src, dest):
        return pltpu.make_async_remote_copy(
            src_ref=s2.at[chunk, dest], dst_ref=r2.at[chunk, src],
            send_sem=send2.at[chunk, dest], recv_sem=recv2.at[chunk, src],
            device_id={"chan": dest}, device_id_type=MESH,
        )

    def copy2x(chunk, src, dest):
        return pltpu.make_async_remote_copy(
            src_ref=s2.at[chunk, dest, 1 - y_hi], dst_ref=r2x.at[chunk, src],
            send_sem=send2x.at[chunk, dest], recv_sem=recv2x.at[chunk, src],
            device_id={"grp": other, "chan": dest}, device_id_type=MESH,
        )

    for item in loads[2:]:
        item.wait()

    for chunk in range(chunks):
        def wait1(d, carry):
            pltpu.make_async_copy(r1.at[chunk, d], r1.at[chunk, d], recv1.at[chunk, d]).wait()
            return carry

        lax.fori_loop(0, n_chan, wait1, 0)

        def first(p, carry):
            lane = pl.multiple_of(p * 128, 128)
            samples = [r1[chunk, d, :, pl.ds(lane, 128)].astype(F32) for d in range(n_chan)]
            for c, (re, im) in enumerate(real_dft(samples)):
                cos = tw[c, 0:1, pl.ds(lane, 128)]
                sin = tw[c, 1:2, pl.ds(lane, 128)]
                if im is None:
                    zr, zi = re * cos, -(re * sin)
                else:
                    zr, zi = re * cos + im * sin, im * cos - re * sin
                for base, z in ((0, zr), (block, zi)):
                    lanes = pl.ds(pl.multiple_of(base + lane, 128), 128)
                    high = z.astype(BF16)
                    zh[c, :, lanes] = high
                    zl[c, :, lanes] = (z - high.astype(F32)).astype(BF16)
            return carry

        lax.fori_loop(0, block // 128, first, 0)
        count = (n_half + 1) * rows
        left_h = zh[...].reshape(count, 2 * block)
        left_l = zl[...].reshape(count, 2 * block)
        out = jnp.dot(left_h, bh[...], preferred_element_type=F32)
        out += jnp.dot(left_h, bl[...], preferred_element_type=F32)
        out += jnp.dot(left_l, bh[...], preferred_element_type=F32)
        for c in range(n_half + 1):
            piece = out[c * rows : (c + 1) * rows].astype(BF16)
            s2[chunk, c, 0] = piece[:, 0:128]
            s2[chunk, c, 1] = piece[:, 128:256]
            if 0 < c < n_half:
                s2[chunk, n_chan - c, 0] = piece[:, 256:384]
                s2[chunk, n_chan - c, 1] = piece[:, 384:512]

        def start2x(k, carry):
            copy2x(chunk, me, peer_of(k)).start()
            return carry

        def start2(k, carry):
            dest = peer_of(k)

            @pl.when(dest != me)
            def _():
                copy2(chunk, me, dest).start()

            return carry

        lax.fori_loop(0, n_chan, start2x, 0)
        lax.fori_loop(0, n_chan, start2, 0)
        pltpu.make_async_copy(s2.at[chunk, me], r2.at[chunk, me], recv2.at[chunk, me]).start()

    low_lane = lax.broadcasted_iota(jnp.int32, (sig, 128), 1) < 64

    def swap(a, b):
        re = jnp.where(low_lane, a, pltpu.roll(b, 64, 1))
        im = jnp.where(low_lane, pltpu.roll(a, 64, 1), b)
        return jnp.concatenate([re, im], 0).T

    def copyq(src_ref, chunk, slot, sem, dest_grp):
        return pltpu.make_async_remote_copy(
            src_ref=src_ref, dst_ref=slots_ref.at[slot, chunk], send_sem=sem, recv_sem=recvq.at[chunk, slot],
            device_id={"grp": dest_grp}, device_id_type=MESH,
        )

    half_rows = 64 * part
    sends = []
    relays = []

    def own_blocks(chunk):
        def turn(s, carry):
            for q in range(quarters):
                e = quarters * s + q
                pltpu.make_async_copy(r2.at[chunk, e], r2.at[chunk, e], recv2.at[chunk, e]).wait()
            low = r2[chunk, pl.ds(quarters * s, quarters), 0].reshape(sig, 128).astype(F32)
            high = r2[chunk, pl.ds(quarters * s, quarters), 1].reshape(sig, 128).astype(F32)
            t32[chunk, pl.ds(s, 128, stride=part), :] = swap(low, high)
            return carry

        lax.fori_loop(0, part, turn, 0)

        def pack(i, carry):
            at = pl.ds(pl.multiple_of(i * 128, 128), 128)
            tn[chunk, at] = t32[chunk, at, :].astype(BF16)
            return carry

        lax.fori_loop(0, 2 * half_rows // 128, pack, 0)
        for dx in range(1, n_x):
            dest_x = lax.rem(x + dx, n_x)
            dest = y_hi * plane + dest_x * 2 + core
            upper = (dest_x > x).astype(jnp.int32)
            sends.append(copyq(
                tn.at[chunk, pl.ds(pl.multiple_of(upper * half_rows, half_rows), half_rows)],
                chunk, gid, sendq.at[chunk, dx - 1], dest,
            ))
            sends[-1].start()
        sends.append(copyq(
            tn.at[chunk, pl.ds(pl.multiple_of((1 - core) * half_rows, half_rows), half_rows)],
            chunk, gid, sendq.at[chunk, n_x - 1], sib,
        ))
        sends[-1].start()

    def cross_blocks(chunk):
        def turnx(i, carry):
            for q in range(2 * quarters):
                e = 2 * quarters * i + q
                pltpu.make_async_copy(r2x.at[chunk, e], r2x.at[chunk, e], recv2x.at[chunk, e]).wait()
            first_s = r2x[chunk, pl.ds(2 * quarters * i, quarters)].reshape(sig, 128).astype(F32)
            second_s = r2x[chunk, pl.ds(2 * quarters * i + quarters, quarters)].reshape(sig, 128).astype(F32)
            both = swap(first_s, second_s)
            t32x[pl.ds(2 * i, 64, stride=part), :] = both[:64]
            t32x[pl.ds(2 * i + 1, 64, stride=part), :] = both[64:]
            return carry

        lax.fori_loop(0, part // 2, turnx, 0)

        def packx(i, carry):
            at = pl.ds(pl.multiple_of(i * 128, 128), 128)
            tx[chunk, at] = t32x[at, :].astype(BF16)
            return carry

        lax.fori_loop(0, half_rows // 128, packx, 0)
        for dx in range(1, n_x):
            dest = y_hi * plane + lax.rem(x + dx, n_x) * 2 + core
            sends.append(copyq(tx.at[chunk], chunk, other, sendq.at[chunk, n_x + dx - 1], dest))
            sends[-1].start()
        sends.append(copyq(tx.at[chunk], chunk, other, sendq.at[chunk, 2 * n_x - 1], sib))
        sends[-1].start()
        pltpu.make_async_copy(tx.at[chunk], slots_ref.at[other, chunk], recvq.at[chunk, other]).start()

    def relay(chunk, side):
        for dx in (1, 3, 2):
            source = lax.rem(y_hi + side, 2) * plane + lax.rem(x + n_x - dx, n_x) * 2 + core
            copyq(tx.at[chunk], chunk, source, keep_sem, sib).wait_recv()
            relays.append(copyq(
                slots_ref.at[source, chunk], chunk, source,
                relay_sem.at[chunk, side * (n_x - 1) + dx - 1], sib,
            ))
            relays[-1].start()

    for chunk in range(chunks):
        cross_blocks(chunk)
        if chunk > 0:
            relay(chunk - 1, 1)
        own_blocks(chunk)
        if chunk > 0:
            relay(chunk - 1, 0)

    per = 8 * part

    def prepare(b, carry):
        at = pl.ds(pl.multiple_of(b * per, per), per)
        both = jnp.concatenate([t32[chunk, at, :] for chunk in range(chunks)], 0).T.astype(BF16)
        left[b, :, 0:128] = both[:64]
        left[b, :, 128:256] = both[64:]
        return carry

    lax.fori_loop(0, 16, prepare, 0)
    keep = pltpu.make_async_copy(left, left_ref, keep_sem)
    keep.start()

    relay(chunks - 1, 1)
    relay(chunks - 1, 0)
    for chunk in range(chunks):
        for side in range(2):
            for dx in range(n_x):
                slot = lax.rem(y_hi + side, 2) * plane + lax.rem(x + dx, n_x) * 2 + (1 - core)
                copyq(tx.at[chunk], chunk, slot, keep_sem, sib).wait_recv()
        pltpu.make_async_copy(tx.at[chunk], slots_ref.at[other, chunk], recvq.at[chunk, other]).wait()
    keep.wait()
    for item in sends + relays:
        item.wait_send()

    for chunk in range(chunks):
        def drain(k, carry):
            dest = lax.rem(me + k, n_chan)

            @pl.when(k > 0)
            def _():
                copy1(chunk, me, dest).wait_send()
                copy2(chunk, me, dest).wait_send()

            copy2x(chunk, me, dest).wait_send()
            return carry

        lax.fori_loop(0, n_chan, drain, 0)


def correlate_kernel(
    chunks, spec, plan_ref, left_ref, slots_ref, out_ref, mine, theirs, out, wide, left, left_sem, slot_sem, out_sem
):
    rounds = out.shape[0]
    part = spec // chunks
    per = 8 * part
    gid = lax.axis_index("grp")
    load = pltpu.make_async_copy(left_ref, mine, left_sem)
    load.start()
    fetches = []
    for r in range(rounds):
        fetches.append(pltpu.make_async_copy(slots_ref.at[plan_ref[r, gid]], theirs.at[r], slot_sem.at[r]))
        fetches[-1].start()
    lane_j = lax.rem(lax.broadcasted_iota(jnp.int32, (8, 128), 1), per) // part
    mask = lane_j == lax.broadcasted_iota(jnp.int32, (8, 128), 0)
    low_lane = lax.broadcasted_iota(jnp.int32, (128, 128), 1) < 64
    load.wait()

    def store(r, i):
        at = pl.ds(pl.multiple_of(i * 16, 16), 16)
        return pltpu.make_async_copy(out.at[r, :, at], out_ref.at[r, :, at], out_sem.at[r, i])

    for r in range(rounds):
        fetches[r].wait()
        base = (gid > plan_ref[r, gid]).astype(jnp.int32) * 8

        def step(i, carry):
            results = []
            for b in range(2):
                wide[b] = mine[base + 2 * i + b].astype(F32)
                for a in range(0, 64, 2):
                    for lane in (0, 128):
                        pair = [
                            jnp.where(mask, jnp.broadcast_to(wide[b, a + k : a + k + 1, lane : lane + 128], (8, 128)), 0.0)
                            for k in range(2)
                        ]
                        left[b, 8 * a : 8 * a + 16, lane : lane + 128] = jnp.concatenate(pair, 0).astype(BF16)
                at = pl.ds(pl.multiple_of((2 * i + b) * per, per), per)
                stack = jnp.concatenate([theirs[r, c, at, :] for c in range(chunks)], 0).astype(F32) * (1.0 / spec)
                right = jnp.concatenate(
                    [jnp.where(low_lane, stack, -stack), pltpu.roll(stack, 64, 1)], 0
                ).astype(BF16)
                product = jnp.dot(left[b], right, preferred_element_type=F32)
                results.append(product.reshape(64, 8, 128))
            out[r, :, pl.ds(pl.multiple_of(i * 16, 16), 16), :] = jnp.concatenate(results, 1).astype(BF16)
            store(r, i).start()
            return carry

        lax.fori_loop(0, 4, step, 0)
    for r in range(rounds):
        for i in range(4):
            store(r, i).wait()


def solution(mesh):
    n_chan = mesh.shape["chan"]
    n_grp = mesh.shape["grp"]
    plane = n_grp // 2
    n_x = plane // 2
    chunks = 2

    def local(voltages, plan):
        sig, frames, block = voltages.shape
        spec = frames - TAPS + 1
        part = spec // chunks
        fft_len = block * n_chan
        rows = sig * part // n_chan
        n_c = n_chan // 2 + 1
        rounds = plan.shape[0]
        table = jnp.asarray(coeff_table(fft_len, n_chan))
        twiddle = jnp.asarray(twiddle_table(fft_len, n_chan))
        high, low = second_matrix(fft_len, block)
        anyspace = pl.BlockSpec(memory_space=pl.ANY)
        dma = pltpu.SemaphoreType.DMA
        left, slots = pl.pallas_call(
            functools.partial(exchange_kernel, (n_chan, plane, sig, spec, block, chunks)),
            out_shape=(
                jax.ShapeDtypeStruct((16, 64, 256), BF16),
                jax.ShapeDtypeStruct((n_grp, chunks, 64 * part, 128), BF16),
            ),
            in_specs=[anyspace] * 5,
            out_specs=(anyspace, anyspace),
            scratch_shapes=[
                pltpu.VMEM((frames, sig, block), jnp.int32),
                pltpu.VMEM((frames, sig, block), F32),
                pltpu.VMEM((TAPS, block), F32),
                pltpu.VMEM((n_c, 2, block), F32),
                pltpu.VMEM((2 * block, 2 * block), BF16),
                pltpu.VMEM((2 * block, 2 * block), BF16),
                pltpu.VMEM((chunks, n_chan, rows, block), BF16),
                pltpu.VMEM((chunks, n_chan, rows, block), BF16),
                pltpu.VMEM((n_c, rows, 2 * block), BF16),
                pltpu.VMEM((n_c, rows, 2 * block), BF16),
                pltpu.VMEM((chunks, n_chan, 2, rows, 128), BF16),
                pltpu.VMEM((chunks, n_chan, 2, rows, 128), BF16),
                pltpu.VMEM((chunks, n_chan, rows, 128), BF16),
                pltpu.VMEM((chunks, 128 * part, 128), F32),
                pltpu.VMEM((64 * part, 128), F32),
                pltpu.VMEM((chunks, 128 * part, 128), BF16),
                pltpu.VMEM((chunks, 64 * part, 128), BF16),
                pltpu.VMEM((16, 64, 256), BF16),
                dma((5,)),
                dma((chunks, n_chan)), dma((chunks, n_chan)), dma((chunks, n_chan)),
                dma((chunks, n_chan)), dma((chunks, n_chan)), dma((chunks, n_chan)),
                dma, dma((chunks, 2 * n_x)), dma((chunks, n_grp)), dma((chunks, 2 * n_x)),
            ],
            compiler_params=pltpu.CompilerParams(
                collective_id=0, has_side_effects=True, vmem_limit_bytes=56 * 1024 * 1024
            ),
            cost_estimate=pl.CostEstimate(
                flops=10**9, bytes_accessed=10**7, transcendentals=0
            ),
        )(voltages.transpose(1, 0, 2), table, twiddle, jnp.asarray(high), jnp.asarray(low))
        return pl.pallas_call(
            functools.partial(correlate_kernel, chunks, spec),
            out_shape=jax.ShapeDtypeStruct((rounds, sig, 64, 2 * sig), BF16),
            in_specs=[pl.BlockSpec(memory_space=pltpu.SMEM), anyspace, anyspace],
            out_specs=anyspace,
            scratch_shapes=[
                pltpu.VMEM((16, 64, 256), BF16),
                pltpu.VMEM((rounds, chunks, 64 * part, 128), BF16),
                pltpu.VMEM((rounds, sig, 64, 128), BF16),
                pltpu.VMEM((2, 64, 256), F32),
                pltpu.VMEM((2, 512, 256), BF16),
                dma, dma((rounds,)), dma((rounds, 4)),
            ],
            compiler_params=pltpu.CompilerParams(vmem_limit_bytes=60 * 1024 * 1024),
        )(plan, left, slots)

    in_specs = (P("grp", None, "chan"), P())
    out_specs = P(None, "grp", "chan", None)
    return jax.shard_map(local, mesh=mesh, in_specs=in_specs, out_specs=out_specs, check_vma=False)
```

time: 99.2 us -> 82.1 us (0.83)
  the two profiles are of different devices: /device:TPU:9 before, /device:TPU:1 now
where the time goes in v2:
time: 82.1 us; the launch traced here: 81.9 us
  Pallas kernels  81.9 us (100%)
    pallas_call x1, Pallas kernels, local(): pl.pallas_call(functools.partial(exchange_kernel, (n_chan, plane, sig, sp...  74.7 us
    pallas_call x1, Pallas kernels, local(): pl.pallas_call(functools.partial(correlate_kernel, chunks, spec), out_sha...  7.2 us

profile of v2, /device:TPU:1, one launch (start us, length us, event | category | flops | bytes accessed | tf_op | source)
XLA Modules:
  0.0 81.9 jit_solution(1562803247657303875)
XLA Ops:
  0.0 74.7 %shard_map.64 = (bf16[16,64,256]{2,1,0:T(8,128)(2,1)}, bf16[16,2,512,128]{3,2,1,0:T(8,128)(2,1)}) custom-call(s32[31,64,256]{2,1,0:T(8,128)} %bitcast.1, f32[32,16,256]{2,1,0:T(8,128)} %constant.8.clone.coeff_ref, f32[17,2,256]{2,1,0:T(2,128)} %constant.9.clone.tw_ref, bf16[512,512]{1,0:T(8,128)(2,1)} %constant.10.clone.bh_ref, ...), custom_call_target="tpu_custom_call" | custom-call | flops 1000000000 | bytes 10000000 | tf_op jit(solution)/shard_map/pallas_call | solution.py:477
  74.7 7.2 %shard_map.65 = bf16[3,64,64,128]{3,2,1,0:T(8,128)(2,1)} custom-call(s32[3,16]{1,0:T(4,128)} %plan_ref.1, bf16[16,64,256]{2,1,0:T(8,128)(2,1)} %get-tuple-element.7.left_ref, bf16[16,2,512,128]{3,2,1,0:T(8,128)(2,1)} %get-tuple-element.8.slots_ref), custom_call_target="tpu_custom_call" | custom-call | tf_op jit(solution)/shard_map/pallas_call | solution.py:516

commit v3 on v2

--- a/solution.py
+++ b/solution.py
@@ -146,6 +146,13 @@
         y = lax.rem(me // 8 + k + k // 8, n_chan // 8)
         return y * 8 + z
 
+    def peer_from(k):
+        step = lax.rem(k, 8)
+        hop = (step // 2 + 1) * (1 - 2 * lax.rem(step, 2)) * (1 - step // 7)
+        z = lax.rem(lax.rem(me, 8) - hop + 8, 8)
+        y = lax.rem(me // 8 - lax.rem(k + k // 8, n_chan // 8) + n_chan // 8, n_chan // 8)
+        return y * 8 + z
+
     def fir(chunk):
         def body(s, carry):
             for lane in range(0, block, 128):
@@ -181,13 +188,24 @@
         pltpu.make_async_copy(filt.at[chunk, me], r1.at[chunk, me], recv1.at[chunk, me]).start()
 
     widen(0, part + TAPS - 1)
+    def wait1(chunk, lo, hi):
+        def body(k, carry):
+            d = peer_from(k)
+            pltpu.make_async_copy(r1.at[chunk, d], r1.at[chunk, d], recv1.at[chunk, d]).wait()
+            return carry
+
+        lax.fori_loop(lo, hi, body, 0)
+
+    widen(0, part + TAPS - 1)
     fir(0)
     pl.semaphore_wait(barrier, 2 * n_chan - 1 + n_x)
     start1(0)
-    for chunk in range(1, chunks):
-        widen(chunk * part + TAPS - 1, (chunk + 1) * part + TAPS - 1)
-        fir(chunk)
-        start1(chunk)
+    widen(part + TAPS - 1, spec + TAPS - 1)
+    fir(1)
+    for item in loads[2:]:
+        item.wait()
+    start1(1)
+    wait1(0, 0, n_chan)
 
     n_half = n_chan // 2
 
@@ -205,16 +223,7 @@
             device_id={"grp": other, "chan": dest}, device_id_type=MESH,
         )
 
-    for item in loads[2:]:
-        item.wait()
-
-    for chunk in range(chunks):
-        def wait1(d, carry):
-            pltpu.make_async_copy(r1.at[chunk, d], r1.at[chunk, d], recv1.at[chunk, d]).wait()
-            return carry
-
-        lax.fori_loop(0, n_chan, wait1, 0)
-
+    def transform(chunk):
         def first(p, carry):
             lane = pl.multiple_of(p * 128, 128)
             samples = [r1[chunk, d, :, pl.ds(lane, 128)].astype(F32) for d in range(n_chan)]
@@ -247,11 +256,15 @@
                 s2[chunk, n_chan - c, 0] = piece[:, 256:384]
                 s2[chunk, n_chan - c, 1] = piece[:, 384:512]
 
-        def start2x(k, carry):
+    def start2x(chunk):
+        def body(k, carry):
             copy2x(chunk, me, peer_of(k)).start()
             return carry
 
-        def start2(k, carry):
+        lax.fori_loop(0, n_chan, body, 0)
+
+    def start2(chunk):
+        def body(k, carry):
             dest = peer_of(k)
 
             @pl.when(dest != me)
@@ -260,8 +273,7 @@
 
             return carry
 
-        lax.fori_loop(0, n_chan, start2x, 0)
-        lax.fori_loop(0, n_chan, start2, 0)
+        lax.fori_loop(0, n_chan, body, 0)
         pltpu.make_async_copy(s2.at[chunk, me], r2.at[chunk, me], recv2.at[chunk, me]).start()
 
     low_lane = lax.broadcasted_iota(jnp.int32, (sig, 128), 1) < 64
@@ -352,13 +364,19 @@
             ))
             relays[-1].start()
 
-    for chunk in range(chunks):
-        cross_blocks(chunk)
-        if chunk > 0:
-            relay(chunk - 1, 1)
-        own_blocks(chunk)
-        if chunk > 0:
-            relay(chunk - 1, 0)
+    transform(0)
+    start2x(0)
+    start2(0)
+    wait1(1, 0, n_chan)
+    transform(1)
+    cross_blocks(0)
+    start2x(1)
+    own_blocks(0)
+    start2(1)
+    cross_blocks(1)
+    relay(0, 1)
+    own_blocks(1)
+    relay(0, 0)
 
     per = 8 * part
 

time: 82.1 us -> 77.7 us (0.946)
  Pallas kernels: 81.9 us -> 77.5 us
    pallas_call x1, Pallas kernels: 74.7 us -> 70.3 us  [local(): pl.pallas_call(functools.partial(exchange_kernel, (n_chan, plane, sig, sp...]
where the time goes in v3:
time: 77.7 us; the launch traced here: 77.5 us
  Pallas kernels  77.5 us (100%)
    pallas_call x1, Pallas kernels, local(): pl.pallas_call(functools.partial(exchange_kernel, (n_chan, plane, sig, sp...  70.3 us
    pallas_call x1, Pallas kernels, local(): pl.pallas_call(functools.partial(correlate_kernel, chunks, spec), out_sha...  7.21 us

profile of v3, /device:TPU:1, one launch (start us, length us, event | category | flops | bytes accessed | tf_op | source)
XLA Modules:
  0.0 77.5 jit_solution(3726807665855559753)
XLA Ops:
  0.0 70.3 %shard_map.64 = (bf16[16,64,256]{2,1,0:T(8,128)(2,1)}, bf16[16,2,512,128]{3,2,1,0:T(8,128)(2,1)}) custom-call(s32[31,64,256]{2,1,0:T(8,128)} %bitcast.1, f32[32,16,256]{2,1,0:T(8,128)} %constant.8.clone.coeff_ref, f32[17,2,256]{2,1,0:T(2,128)} %constant.9.clone.tw_ref, bf16[512,512]{1,0:T(8,128)(2,1)} %constant.10.clone.bh_ref, ...), custom_call_target="tpu_custom_call" | custom-call | flops 1000000000 | bytes 10000000 | tf_op jit(solution)/shard_map/pallas_call | solution.py:495
  70.3 7.2 %shard_map.65 = bf16[3,64,64,128]{3,2,1,0:T(8,128)(2,1)} custom-call(s32[3,16]{1,0:T(4,128)} %plan_ref.1, bf16[16,64,256]{2,1,0:T(8,128)(2,1)} %get-tuple-element.7.left_ref, bf16[16,2,512,128]{3,2,1,0:T(8,128)(2,1)} %get-tuple-element.8.slots_ref), custom_call_target="tpu_custom_call" | custom-call | tf_op jit(solution)/shard_map/pallas_call | solution.py:534

commit v4 on v3

--- a/solution.py
+++ b/solution.py
@@ -86,7 +86,7 @@
     v_ref, coeff_ref, tw_ref, bh_ref, bl_ref,
     left_ref, slots_ref,
     volts, vf, coeff, tw, bh, bl, filt, r1, zh, zl, s2, r2, r2x, t32, t32x, tn, tx, left,
-    load_sem, send1, recv1, send2, recv2, send2x, recv2x, keep_sem, sendq, recvq, relay_sem,
+    load_sem, send1, recv1, send2, recv2, send2x, recv2x, keep_sem, sendq, recvq, relay_sem, row_sem,
 ):
     n_chan, plane, sig, spec, block, chunks = dims
     part = spec // chunks
@@ -113,17 +113,11 @@
 
     def greet(k, carry):
         peer = lax.rem(me + k, n_chan)
-
-        @pl.when(k > 0)
-        def _():
-            pl.semaphore_signal(barrier, inc=1, device_id={"chan": peer}, device_id_type=MESH)
-
-        pl.semaphore_signal(
-            barrier, inc=1, device_id={"grp": other, "chan": peer}, device_id_type=MESH
-        )
+        pl.semaphore_signal(barrier, inc=1, device_id={"chan": peer}, device_id_type=MESH)
         return carry
 
-    lax.fori_loop(0, n_chan, greet, 0)
+    lax.fori_loop(1, n_chan, greet, 0)
+    pl.semaphore_signal(barrier, inc=1, device_id={"grp": other}, device_id_type=MESH)
     for dx in range(1, n_x):
         dest = y_hi * plane + lax.rem(x + dx, n_x) * 2 + core
         pl.semaphore_signal(barrier, inc=1, device_id={"grp": dest}, device_id_type=MESH)
@@ -198,7 +192,8 @@
 
     widen(0, part + TAPS - 1)
     fir(0)
-    pl.semaphore_wait(barrier, 2 * n_chan - 1 + n_x)
+    pl.semaphore_wait(barrier, n_chan + n_x)
+    pl.semaphore_signal(row_sem, inc=1, device_id={"grp": other}, device_id_type=MESH)
     start1(0)
     widen(part + TAPS - 1, spec + TAPS - 1)
     fir(1)
@@ -365,6 +360,7 @@
             relays[-1].start()
 
     transform(0)
+    pl.semaphore_wait(row_sem, 1)
     start2x(0)
     start2(0)
     wait1(1, 0, n_chan)
@@ -442,31 +438,34 @@
 
     for r in range(rounds):
         fetches[r].wait()
-        base = (gid > plan_ref[r, gid]).astype(jnp.int32) * 8
-
-        def step(i, carry):
-            results = []
+
+    def step(i, carry):
+        for u in range(2):
             for b in range(2):
-                wide[b] = mine[base + 2 * i + b].astype(F32)
+                wide[...] = mine[u * 8 + 2 * i + b].astype(F32)
                 for a in range(0, 64, 2):
                     for lane in (0, 128):
                         pair = [
-                            jnp.where(mask, jnp.broadcast_to(wide[b, a + k : a + k + 1, lane : lane + 128], (8, 128)), 0.0)
+                            jnp.where(mask, jnp.broadcast_to(wide[a + k : a + k + 1, lane : lane + 128], (8, 128)), 0.0)
                             for k in range(2)
                         ]
-                        left[b, 8 * a : 8 * a + 16, lane : lane + 128] = jnp.concatenate(pair, 0).astype(BF16)
+                        left[u, b, 8 * a : 8 * a + 16, lane : lane + 128] = jnp.concatenate(pair, 0).astype(BF16)
+        for r in range(rounds):
+            u = (gid > plan_ref[r, gid]).astype(jnp.int32)
+            results = []
+            for b in range(2):
                 at = pl.ds(pl.multiple_of((2 * i + b) * per, per), per)
                 stack = jnp.concatenate([theirs[r, c, at, :] for c in range(chunks)], 0).astype(F32) * (1.0 / spec)
                 right = jnp.concatenate(
                     [jnp.where(low_lane, stack, -stack), pltpu.roll(stack, 64, 1)], 0
                 ).astype(BF16)
-                product = jnp.dot(left[b], right, preferred_element_type=F32)
+                product = jnp.dot(left[u, b], right, preferred_element_type=F32)
                 results.append(product.reshape(64, 8, 128))
             out[r, :, pl.ds(pl.multiple_of(i * 16, 16), 16), :] = jnp.concatenate(results, 1).astype(BF16)
             store(r, i).start()
-            return carry
-
-        lax.fori_loop(0, 4, step, 0)
+        return carry
+
+    lax.fori_loop(0, 4, step, 0)
     for r in range(rounds):
         for i in range(4):
             store(r, i).wait()
@@ -523,6 +522,7 @@
                 dma((chunks, n_chan)), dma((chunks, n_chan)), dma((chunks, n_chan)),
                 dma((chunks, n_chan)), dma((chunks, n_chan)), dma((chunks, n_chan)),
                 dma, dma((chunks, 2 * n_x)), dma((chunks, n_grp)), dma((chunks, 2 * n_x)),
+                pltpu.SemaphoreType.REGULAR,
             ],
             compiler_params=pltpu.CompilerParams(
                 collective_id=0, has_side_effects=True, vmem_limit_bytes=56 * 1024 * 1024
@@ -540,8 +540,8 @@
                 pltpu.VMEM((16, 64, 256), BF16),
                 pltpu.VMEM((rounds, chunks, 64 * part, 128), BF16),
                 pltpu.VMEM((rounds, sig, 64, 128), BF16),
-                pltpu.VMEM((2, 64, 256), F32),
-                pltpu.VMEM((2, 512, 256), BF16),
+                pltpu.VMEM((64, 256), F32),
+                pltpu.VMEM((2, 2, 512, 256), BF16),
                 dma, dma((rounds,)), dma((rounds, 4)),
             ],
             compiler_params=pltpu.CompilerParams(vmem_limit_bytes=60 * 1024 * 1024),

time: 77.7 us -> 74.8 us (0.963)
  Pallas kernels: 77.5 us -> 74.3 us
    pallas_call x1, Pallas kernels: 70.3 us -> 67.9 us  [local(): pl.pallas_call(functools.partial(exchange_kernel, (n_chan, plane, sig, sp...]
where the time goes in v4:
time: 74.8 us; the launch traced here: 74.3 us
  Pallas kernels  74.3 us (99%)
    pallas_call x1, Pallas kernels, local(): pl.pallas_call(functools.partial(exchange_kernel, (n_chan, plane, sig, sp...  67.9 us
    pallas_call x1, Pallas kernels, local(): pl.pallas_call(functools.partial(correlate_kernel, chunks, spec), out_sha...  6.44 us

profile of v4, /device:TPU:1, one launch (start us, length us, event | category | flops | bytes accessed | tf_op | source)
XLA Modules:
  0.0 74.3 jit_solution(10553342674820043007)
XLA Ops:
  0.0 67.9 %shard_map.64 = (bf16[16,64,256]{2,1,0:T(8,128)(2,1)}, bf16[16,2,512,128]{3,2,1,0:T(8,128)(2,1)}) custom-call(s32[31,64,256]{2,1,0:T(8,128)} %bitcast.1, f32[32,16,256]{2,1,0:T(8,128)} %constant.8.clone.coeff_ref, f32[17,2,256]{2,1,0:T(2,128)} %constant.9.clone.tw_ref, bf16[512,512]{1,0:T(8,128)(2,1)} %constant.10.clone.bh_ref, ...), custom_call_target="tpu_custom_call" | custom-call | flops 1000000000 | bytes 10000000 | tf_op jit(solution)/shard_map/pallas_call | solution.py:494
  67.9 6.4 %shard_map.65 = bf16[3,64,64,128]{3,2,1,0:T(8,128)(2,1)} custom-call(s32[3,16]{1,0:T(4,128)} %plan_ref.1, bf16[16,64,256]{2,1,0:T(8,128)(2,1)} %get-tuple-element.7.left_ref, bf16[16,2,512,128]{3,2,1,0:T(8,128)(2,1)} %get-tuple-element.8.slots_ref), custom_call_target="tpu_custom_call" | custom-call | tf_op jit(solution)/shard_map/pallas_call | solution.py:534

commit v5 on v4

--- a/solution.py
+++ b/solution.py
@@ -369,8 +369,8 @@
     start2x(1)
     own_blocks(0)
     start2(1)
+    relay(0, 1)
     cross_blocks(1)
-    relay(0, 1)
     own_blocks(1)
     relay(0, 0)
 

time: 74.8 us -> 74.8 us (level)
  no operation moved by 1% of the time
where the time goes in v5:
time: 74.8 us; the launch traced here: 74.3 us
  Pallas kernels  74.3 us (99%)
    pallas_call x1, Pallas kernels, local(): pl.pallas_call(functools.partial(exchange_kernel, (n_chan, plane, sig, sp...  67.9 us
    pallas_call x1, Pallas kernels, local(): pl.pallas_call(functools.partial(correlate_kernel, chunks, spec), out_sha...  6.44 us

profile of v5, /device:TPU:1, one launch (start us, length us, event | category | flops | bytes accessed | tf_op | source)
XLA Modules:
  0.0 74.3 jit_solution(15368386347557679612)
XLA Ops:
  0.0 67.9 %shard_map.64 = (bf16[16,64,256]{2,1,0:T(8,128)(2,1)}, bf16[16,2,512,128]{3,2,1,0:T(8,128)(2,1)}) custom-call(s32[31,64,256]{2,1,0:T(8,128)} %bitcast.1, f32[32,16,256]{2,1,0:T(8,128)} %constant.8.clone.coeff_ref, f32[17,2,256]{2,1,0:T(2,128)} %constant.9.clone.tw_ref, bf16[512,512]{1,0:T(8,128)(2,1)} %constant.10.clone.bh_ref, ...), custom_call_target="tpu_custom_call" | custom-call | flops 1000000000 | bytes 10000000 | tf_op jit(solution)/shard_map/pallas_call | solution.py:494
  67.9 6.4 %shard_map.65 = bf16[3,64,64,128]{3,2,1,0:T(8,128)(2,1)} custom-call(s32[3,16]{1,0:T(4,128)} %plan_ref.1, bf16[16,64,256]{2,1,0:T(8,128)(2,1)} %get-tuple-element.7.left_ref, bf16[16,2,512,128]{3,2,1,0:T(8,128)(2,1)} %get-tuple-element.8.slots_ref), custom_call_target="tpu_custom_call" | custom-call | tf_op jit(solution)/shard_map/pallas_call | solution.py:534
